TPU v7x, 32 devices: a whole 2x2x4 slice. The times are simulated.
32 devices in a mesh: seq: 16 (over z, y, core), kv: 2 (over x).
Axes of the slice: x: 2, y: 2, z: 4, core: 2. Of those that a mesh axis runs over, the one named last changes fastest.
Arguments:
- queries: bfloat16 [4096, 32, 128], P('seq', 'kv'), may hold values from -6 to 6
- keys: bfloat16 [4096, 16, 128], P('seq', 'kv'), may hold values from -6 to 6
- values: bfloat16 [4096, 16, 128], P('seq', 'kv'), may hold values from -6 to 6
- output_gradient: bfloat16 [4096, 32, 128], P('seq', 'kv'), may hold values from -288 to 288
- window_start: int32 [4096], P('seq'), may hold values from 0 to 4095, as said below
- query_gain: float32 [128], replicated, may hold values from 0.1 to 1.9
- key_gain: float32 [128], replicated, may hold values from 0.1 to 1.9
Outputs:
- query_grad: bfloat16 [4096, 32, 128], P('seq', 'kv')
- key_grad: bfloat16 [4096, 16, 128], P('seq', 'kv')
- value_grad: bfloat16 [4096, 16, 128], P('seq', 'kv')
- query_gain_grad: float32 [128], replicated
- key_gain_grad: float32 [128], replicated
Inputs may be any that keep to these rules, and one draw needn't show every extreme that they name: window_start[t] = max(first position of token t's document, t - 1023); documents are runs of consecutive tokens, the last token begins a document of its own, and t - window_start[t] equals 1023 for some token.
All inputs are finite; a program needn't handle non-finite values.
Results may differ from a plain program's by a relative error of at most 0.014.
Values may be sent and summed in bfloat16 or wider, within the bound.
A program may use at most 128 MiB of HBM per device.

v0:
```python
import functools
import math

import jax
import jax.numpy as jnp
from jax import lax
from jax.experimental import pallas as pl
from jax.experimental.pallas import tpu as pltpu
from jax.sharding import PartitionSpec as P

WINDOW_LENGTH = 1024

attn_scale = 168.0 ** (-0.5)
norm_eps = 1e-06
rope_base = 10000.0
log2_e = math.log2(math.e)
f32 = jnp.float32
bf16 = jnp.bfloat16


def hop(value, axis, step):
    count = lax.axis_size(axis)
    initial, last = (max(0, -step), min(count, count - step))
    return lax.ppermute(value, axis, [(source, source + step) for source in range(initial, last)])


def rotary_tables(positions, head_width):
    half_width = head_width // 2
    frequency = rope_base ** (-(jnp.arange(half_width, dtype=f32) * 2.0) / head_width)
    angles = positions.astype(f32)[:, None] * frequency[None, :]
    cos, sin = jnp.cos(angles), jnp.sin(angles)
    return (jnp.concatenate([cos, cos], axis=-1), jnp.concatenate([-sin, sin], axis=-1))


def swap_halves(x):
    half = x.shape[-1] // 2
    return jnp.concatenate([x[:, half:], x[:, :half]], axis=-1)


def normalize(x, gain):
    x = x.astype(f32)
    inv = lax.rsqrt(jnp.mean(x * x, axis=-1, keepdims=True) + norm_eps)
    unit = x * inv
    return unit, inv, unit * gain


def norm_back(rot_grad, unit, inv, gain, cos, sin):
    grad = rot_grad * cos - swap_halves(rot_grad) * sin
    grad_unit = grad * gain
    out = inv * (grad_unit - unit * jnp.mean(grad_unit * unit, axis=-1, keepdims=True))
    part = grad * unit
    return out, jnp.sum(part.reshape(part.shape[0] // 8, 8, part.shape[1]), axis=0)


def dot(a, b, ca, cb):
    return lax.dot_general(a, b, (((ca,), (cb,)), ((), ())), preferred_element_type=f32)


def prep_kernel(k_ref, v_ref, gain_ref, cos_ref, sin_ref, kv_ref):
    heads, _, rows, width = kv_ref.shape
    for g in range(heads):
        cols = slice(g * width, (g + 1) * width)
        _, _, normed = normalize(k_ref[:, cols], gain_ref[...])
        rot = normed * cos_ref[...] + swap_halves(normed) * sin_ref[...]
        kv_ref[g, 0] = rot.astype(bf16)
        kv_ref[g, 1] = v_ref[:, cols]


def attn_kernel(blocks, group, *refs):
    q_ref, do_ref, low_ref, gain_ref, cos_ref, sin_ref = refs[:6]
    kv = refs[6 : 6 + blocks]
    dq_ref, part_ref = refs[6 + blocks : 8 + blocks]
    terms = refs[8 + blocks : 8 + 2 * blocks]
    e_scr, gw_scr = refs[8 + 2 * blocks :]
    rows, width = cos_ref.shape
    cos, sin, gain = cos_ref[...], sin_ref[...], gain_ref[...]
    rots, saved = [], []
    for h in range(group):
        unit, inv, normed = normalize(q_ref[:, h * width : (h + 1) * width], gain)
        rots.append((normed * cos + swap_halves(normed) * sin).astype(bf16))
    q = jnp.concatenate(rots, axis=0)
    do = jnp.concatenate([do_ref[:, h * width : (h + 1) * width] for h in range(group)], axis=0)
    low = low_ref[...]
    shape = (rows, rows * group)
    key_iota = lax.broadcasted_iota(jnp.int32, shape, 0)
    query_iota = lax.rem(lax.broadcasted_iota(jnp.int32, (1, rows * group), 1), rows)
    total = jnp.zeros((1, rows * group), f32)
    for j in range(blocks):
        s = dot(kv[j][0, 0], q, 1, 1)
        e = jnp.exp2(s * (attn_scale * log2_e))
        seen = key_iota >= low - j * rows
        if j == blocks - 1:
            seen = seen & (key_iota <= query_iota)
        e = jnp.where(seen, e, 0.0)
        total = total + jnp.sum(e, axis=0, keepdims=True)
        e_scr[j] = e
    inv_total = 1.0 / total
    delta = jnp.zeros((1, rows * group), f32)
    for j in range(blocks):
        w = e_scr[j] * inv_total
        wb = w.astype(bf16)
        gw = dot(kv[j][0, 1], do, 1, 1)
        delta = delta + jnp.sum(wb.astype(f32) * gw, axis=0, keepdims=True)
        gw_scr[j] = gw
        e_scr[j] = w
        terms[j][0, 1] = dot(wb, do, 1, 0).astype(terms[j].dtype)
    dq_t = jnp.zeros((width, rows * group), f32)
    for j in range(blocks):
        gs = (e_scr[j] * (gw_scr[j] - delta) * attn_scale).astype(bf16)
        dq_t = dq_t + dot(kv[j][0, 0], gs, 0, 0)
        terms[j][0, 0] = dot(gs, q, 1, 0).astype(terms[j].dtype)
    dq = dq_t.T
    part = jnp.zeros((8, width), f32)
    for h in range(group):
        unit, inv, _ = normalize(q_ref[:, h * width : (h + 1) * width], gain)
        out, p = norm_back(dq[h * rows : (h + 1) * rows], unit, inv, gain, cos, sin)
        dq_ref[:, h * width : (h + 1) * width] = out.astype(bf16)
        part = part + p
    part_ref[0] = part


def final_kernel(carry_ref, term_ref, k_ref, gain_ref, cos_ref, sin_ref, dk_ref, dv_ref, part_ref):
    heads, _, rows, width = term_ref.shape
    gain, cos, sin = gain_ref[...], cos_ref[...], sin_ref[...]
    part = jnp.zeros((8, width), f32)
    for g in range(heads):
        cols = slice(g * width, (g + 1) * width)
        unit, inv, _ = normalize(k_ref[:, cols], gain)
        dk = carry_ref[g, 0].astype(f32) + term_ref[g, 0]
        out, p = norm_back(dk, unit, inv, gain, cos, sin)
        dk_ref[:, cols] = out.astype(bf16)
        dv_ref[:, cols] = (carry_ref[g, 1].astype(f32) + term_ref[g, 1]).astype(bf16)
        part = part + p
    part_ref[...] = part


def body(queries, keys, values, output_gradient, window_start, query_gain, key_gain):
    rows, q_heads, width = queries.shape
    kv_heads = keys.shape[1]
    group = q_heads // kv_heads
    reach = WINDOW_LENGTH // rows
    blocks = reach + 1
    first = lax.axis_index("seq") * rows
    cos, sin = rotary_tables(first + jnp.arange(rows, dtype=jnp.int32), width)
    low = jnp.tile(window_start - first + reach * rows, group)[None, :]
    q2 = queries.reshape(rows, q_heads * width)
    do2 = output_gradient.reshape(rows, q_heads * width)
    k2 = keys.reshape(rows, kv_heads * width)
    v2 = values.reshape(rows, kv_heads * width)
    q_gain, k_gain = query_gain[None, :], key_gain[None, :]
    params = pltpu.CompilerParams(vmem_limit_bytes=56 * 1024 * 1024)
    kv_shape = (kv_heads, 2, rows, width)
    kv = pl.pallas_call(
        prep_kernel, out_shape=jax.ShapeDtypeStruct(kv_shape, bf16), compiler_params=params
    )(k2, v2, k_gain, cos, sin)
    held = [kv]
    for _ in range(reach):
        held.append(hop(held[-1], "seq", 1))
    held = held[::-1]

    whole = lambda a: pl.BlockSpec(a.shape, lambda g: (0,) * a.ndim)
    head = pl.BlockSpec((1, 2, rows, width), lambda g: (g, 0, 0, 0))
    pair = pl.BlockSpec((rows, group * width), lambda g: (0, g))
    outs = pl.pallas_call(
        functools.partial(attn_kernel, blocks, group),
        grid=(kv_heads,),
        in_specs=[pair, pair, whole(low), whole(q_gain), whole(cos), whole(sin)] + [head] * blocks,
        out_specs=[pair, pl.BlockSpec((1, 8, width), lambda g: (g, 0, 0))] + [head] * blocks,
        out_shape=[
            jax.ShapeDtypeStruct(q2.shape, bf16),
            jax.ShapeDtypeStruct((kv_heads, 8, width), f32),
        ]
        + [jax.ShapeDtypeStruct(kv_shape, bf16)] * reach
        + [jax.ShapeDtypeStruct(kv_shape, f32)],
        scratch_shapes=[pltpu.VMEM((blocks, rows, rows * group), f32)] * 2,
        compiler_params=params,
    )(q2, do2, low, q_gain, cos, sin, *held)
    dq, q_part = outs[:2]
    terms = outs[2:]
    carry = terms[0]
    for k in range(reach):
        carry = hop(carry, "seq", -1)
        if k < reach - 1:
            carry = (carry.astype(f32) + terms[k + 1].astype(f32)).astype(bf16)
    dk, dv, k_part = pl.pallas_call(
        final_kernel,
        out_shape=[
            jax.ShapeDtypeStruct(k2.shape, bf16),
            jax.ShapeDtypeStruct(k2.shape, bf16),
            jax.ShapeDtypeStruct((8, width), f32),
        ],
        compiler_params=params,
    )(carry, terms[-1], k2, k_gain, cos, sin)
    parts = jnp.stack([jnp.sum(q_part, axis=(0, 1)), jnp.sum(k_part, axis=0)])
    gains = lax.psum(parts, ("seq", "kv"))
    return (
        dq.reshape(queries.shape),
        dk.reshape(keys.shape),
        dv.reshape(values.shape),
        gains[0],
        gains[1],
    )


def solution(mesh):
    split = P("seq", "kv", None)
    return jax.shard_map(
        body,
        mesh=mesh,
        in_specs=(split, split, split, split, P("seq"), P(), P()),
        out_specs=(split, split, split, P(), P()),
        check_vma=False,
    )
```

profile of v0, /device:TPU:0, one launch (start us, length us, event | category | flops | bytes accessed | tf_op | source)
XLA Modules:
  0.0 224.4 jit_solution(5913006234606817831)
XLA Ops:
  0.7 0.7 add_convert_fusion.3
  1.3 0.5 fusion
  1.9 0.7 pad_maximum_fusion.cos_ref.refs_4_
  2.6 0.8 pad_maximum_fusion.1.sin_ref.refs_5_
  3.4 2.5 %copy_bitcast_fusion.2 = (bf16[256,1024]{1,0:T(8,128)(2,1)}, bf16[256,1024]{1,0:T(8,128)(2,1)}) fusion(bf16[32,8,8,128]{3,2,1,0:T(8,128)(2,1)} %bitcast.38, bf16[32,8,8,128]{3,2,1,0:T(8,128)(2,1)} %bitcast.39), kind=kLoop, calls=%fused_computation.5 | loop fusion | bytes 2097152 | tf_op jit(solution)/shard_map/reshape | solution.py:149
  5.9 3.5 %shard_map.110.refs_10_ = bf16[8,2,256,128]{3,2,1,0:T(8,128)(2,1)} custom-call(bf16[256,1024]{1,0:T(8,128)(2,1)} %get-tuple-element.33.k_ref, bf16[256,1024]{1,0:T(8,128)(2,1)} %get-tuple-element.32.v_ref, f32[1,128]{1,0:T(1,128)} %bitcast.41, f32[256,128]{1,0:T(8,128)} %pad_maximum_fusion.cos_ref.refs_4_, f32[256,128]{1,0:T(8,128)} %pad_maximum_fusion.1.sin_ref.refs_5_), custom_call_target="tpu_custom_call" | custom-call | tf_op jit(solution)/shard_map/pallas_call | solution.py:153
  9.4 2.4 %collective-permute-start = (bf16[8,2,256,128]{3,2,1,0:T(8,128)(2,1)}, bf16[8,2,256,128]{3,2,1,0:T(8,128)(2,1)S(1)}, u32[]{:S(2)}, u32[]{:S(2)}) collective-permute-start(bf16[8,2,256,128]{3,2,1,0:T(8,128)(2,1)} %shard_map.110.refs_10_), channel_id=1, source_target_pairs={{0,2},{2,4},{4,6},{6,8},{8,10},{10,12},{12,14},{14,16},{16,18},{18... | collective-permute-start | bytes 3145736 | tf_op jit(solution)/shard_map/ppermute | solution.py:24
  11.8 2.4 %collective-permute-done.refs_9_ = bf16[8,2,256,128]{3,2,1,0:T(8,128)(2,1)S(1)} collective-permute-done((bf16[8,2,256,128]{3,2,1,0:T(8,128)(2,1)}, bf16[8,2,256,128]{3,2,1,0:T(8,128)(2,1)S(1)}, u32[]{:S(2)}, u32[]{:S(2)}) %collective-permute-start) | collective-permute-done | bytes 1048608 | tf_op jit(solution)/shard_map/ppermute | solution.py:24
  14.2 14.2 %collective-permute-start.1 = (bf16[8,2,256,128]{3,2,1,0:T(8,128)(2,1)S(1)}, bf16[8,2,256,128]{3,2,1,0:T(8,128)(2,1)S(1)}, u32[]{:S(2)}, u32[]{:S(2)}) collective-permute-start(bf16[8,2,256,128]{3,2,1,0:T(8,128)(2,1)S(1)} %collective-permute-done.refs_9_), channel_id=1, source_target_pairs={{0,2},{2,4},{4,6},{6,8},{8,10},{10,12},{12,14},{14,16},{16,18},{18... | collective-permute-start | bytes 3145736 | tf_op jit(solution)/shard_map/ppermute | solution.py:24
  28.4 2.2 collective-permute-done.1.refs_8_
  30.6 13.8 %collective-permute-start.2 = (bf16[8,2,256,128]{3,2,1,0:T(8,128)(2,1)S(1)}, bf16[8,2,256,128]{3,2,1,0:T(8,128)(2,1)S(1)}, u32[]{:S(2)}, u32[]{:S(2)}) collective-permute-start(bf16[8,2,256,128]{3,2,1,0:T(8,128)(2,1)S(1)} %collective-permute-done.1.refs_8_), channel_id=1, source_target_pairs={{0,2},{2,4},{4,6},{6,8},{8,10},{10,12},{12,14},{14,16},{16,18},{18... | collective-permute-start | bytes 3145736 | tf_op jit(solution)/shard_map/ppermute | solution.py:24
  44.4 2.2 collective-permute-done.2.refs_7_
  46.6 13.9 %collective-permute-start.3 = (bf16[8,2,256,128]{3,2,1,0:T(8,128)(2,1)S(1)}, bf16[8,2,256,128]{3,2,1,0:T(8,128)(2,1)S(1)}, u32[]{:S(2)}, u32[]{:S(2)}) collective-permute-start(bf16[8,2,256,128]{3,2,1,0:T(8,128)(2,1)S(1)} %collective-permute-done.2.refs_7_), channel_id=1, source_target_pairs={{0,2},{2,4},{4,6},{6,8},{8,10},{10,12},{12,14},{14,16},{16,18},{18... | collective-permute-start | bytes 3145736 | tf_op jit(solution)/shard_map/ppermute | solution.py:24
  60.5 0.6 copy.14
  61.1 1.8 copy_bitcast_fusion
  62.9 1.0 copy-done.8
  63.9 25.7 %shard_map.111 = (bf16[256,2048]{1,0:T(8,128)(2,1)}, f32[8,8,128]{2,1,0:T(8,128)}, bf16[8,2,256,128]{3,2,1,0:T(8,128)(2,1)}, bf16[8,2,256,128]{3,2,1,0:T(8,128)(...) custom-call(bf16[256,2048]{1,0:T(8,128)(2,1)} %get-tuple-element.35.refs_0_, ...), custom_call_target="tpu_custom_call" | custom-call | tf_op jit(solution)/shard_map/pallas_call | solution.py:164
  89.6 1.4 collective-permute-start.4
  91.1 14.7 %collective-permute-done.4 = bf16[8,2,256,128]{3,2,1,0:T(8,128)(2,1)S(1)} collective-permute-done((bf16[8,2,256,128]{3,2,1,0:T(8,128)(2,1)}, bf16[8,2,256,128]{3,2,1,0:T(8,128)(2,1)S(1)}, u32[]{:S(2)}, u32[]{:S(2)}) %collective-permute-start.4) | collective-permute-done | bytes 1048608 | tf_op jit(solution)/shard_map/ppermute | solution.py:24
  105.7 1.5 add_convert_fusion.2
  107.2 1.4 collective-permute-start.5
  108.7 15.6 %collective-permute-done.5 = bf16[8,2,256,128]{3,2,1,0:T(8,128)(2,1)S(1)} collective-permute-done((bf16[8,2,256,128]{3,2,1,0:T(8,128)(2,1)S(1)}, bf16[8,2,256,128]{3,2,1,0:T(8,128)(2,1)S(1)}, u32[]{:S(2)}, u32[]{:S(2)}) %collective-permute-start.5) | collective-permute-done | bytes 1048608 | tf_op jit(solution)/shard_map/ppermute | solution.py:24
  124.5 1.4 collective-permute-start.6
  126.0 14.8 %collective-permute-done.6 = bf16[8,2,256,128]{3,2,1,0:T(8,128)(2,1)S(1)} collective-permute-done((bf16[8,2,256,128]{3,2,1,0:T(8,128)(2,1)S(1)}, bf16[8,2,256,128]{3,2,1,0:T(8,128)(2,1)S(1)}, u32[]{:S(2)}, u32[]{:S(2)}) %collective-permute-start.6) | collective-permute-done | bytes 1048608 | tf_op jit(solution)/shard_map/ppermute | solution.py:24
  141.2 1.3 collective-permute-start.7
  142.5 1.2 copy.17
  143.7 13.6 %collective-permute-done.7.carry_ref = bf16[8,2,256,128]{3,2,1,0:T(8,128)(2,1)S(1)} collective-permute-done((bf16[8,2,256,128]{3,2,1,0:T(8,128)(2,1)S(1)}, bf16[8,2,256,128]{3,2,1,0:T(8,128)(2,1)S(1)}, u32[]{:S(2)}, u32[]{:S(2)}) %collective-permute-start.7) | collective-permute-done | bytes 1048608 | tf_op jit(solution)/shard_map/ppermute | solution.py:24
  157.3 1.0 copy-done.9
  158.3 4.3 %shard_map.112 = (bf16[256,1024]{1,0:T(8,128)(2,1)}, bf16[256,1024]{1,0:T(8,128)(2,1)}, f32[8,128]{1,0:T(8,128)}) custom-call(bf16[8,2,256,128]{3,2,1,0:T(8,128)(2,1)} %copy-done.9, f32[8,2,256,128]{3,2,1,0:T(8,128)} %get-tuple-element.20.term_ref, bf16[256,1024]{1,0:T(8,128)(2,1)} %get-tuple-element.33.k_ref, f32[1,128]{1,0:T(1,128)} %bitcast.42, ...), custom_call_target="tpu_custom_call" | custom-call | tf_op jit(solution)/shard_map/pallas_call | solution.py:185
  162.6 1.9 copy.18
  164.5 1.9 copy.19
  166.5 57.4 %psum.7 = f32[2,128]{1,0:T(2,128)S(1)} all-reduce(f32[2,128]{1,0:T(2,128)S(1)} %pad_maximum_fusion.2), channel_id=1, replica_groups=mesh['seq'=16,'kv'=2] {'seq','kv'}, use_global_device_ids=true, to_apply=%region_2.0 | all-reduce | flops 256 | bytes 2048 | tf_op jit(solution)/shard_map/psum | solution.py:195
  (31 shorter events, 1.3 us)
Async XLA Ops:
  3.4 57.7 %copy-start.3 = (bf16[256,16,128]{2,1,0:T(8,128)(2,1)S(1)}, bf16[256,16,128]{2,1,0:T(8,128)(2,1)}, u32[]{:S(2)}) copy-start(bf16[256,16,128]{2,1,0:T(8,128)(2,1)} %param.10) | copy-start | bytes 3145732
  3.4 57.7 %copy-start.4 = (bf16[256,16,128]{2,1,0:T(8,128)(2,1)S(1)}, bf16[256,16,128]{2,1,0:T(8,128)(2,1)}, u32[]{:S(2)}) copy-start(bf16[256,16,128]{2,1,0:T(8,128)(2,1)} %param.7) | copy-start | bytes 3145732
  9.4 4.8 %collective-permute-start = (bf16[8,2,256,128]{3,2,1,0:T(8,128)(2,1)}, bf16[8,2,256,128]{3,2,1,0:T(8,128)(2,1)S(1)}, u32[]{:S(2)}, u32[]{:S(2)}) collective-permute-start(bf16[8,2,256,128]{3,2,1,0:T(8,128)(2,1)} %shard_map.110.refs_10_), channel_id=1, source_target_pairs={{0,2},{2,4},{4,6},{6,8},{8,10},{10,12},{12,14},{14,16},{16,18},{18... | collective-permute-start | bytes 3145736 | tf_op jit(solution)/shard_map/ppermute | solution.py:24
  14.2 48.7 %copy-start.5 = (bf16[8,2,256,128]{3,2,1,0:T(8,128)(2,1)}, bf16[8,2,256,128]{3,2,1,0:T(8,128)(2,1)S(1)}, u32[]{:S(2)}) copy-start(bf16[8,2,256,128]{3,2,1,0:T(8,128)(2,1)S(1)} %collective-permute-done.refs_9_) | copy-start | bytes 3145732
  14.2 16.4 %collective-permute-start.1 = (bf16[8,2,256,128]{3,2,1,0:T(8,128)(2,1)S(1)}, bf16[8,2,256,128]{3,2,1,0:T(8,128)(2,1)S(1)}, u32[]{:S(2)}, u32[]{:S(2)}) collective-permute-start(bf16[8,2,256,128]{3,2,1,0:T(8,128)(2,1)S(1)} %collective-permute-done.refs_9_), channel_id=1, source_target_pairs={{0,2},{2,4},{4,6},{6,8},{8,10},{10,12},{12,14},{14,16},{16,18},{18... | collective-permute-start | bytes 3145736 | tf_op jit(solution)/shard_map/ppermute | solution.py:24
  30.6 32.3 %copy-start.6 = (bf16[8,2,256,128]{3,2,1,0:T(8,128)(2,1)}, bf16[8,2,256,128]{3,2,1,0:T(8,128)(2,1)S(1)}, u32[]{:S(2)}) copy-start(bf16[8,2,256,128]{3,2,1,0:T(8,128)(2,1)S(1)} %collective-permute-done.1.refs_8_) | copy-start | bytes 3145732
  30.6 16.0 %collective-permute-start.2 = (bf16[8,2,256,128]{3,2,1,0:T(8,128)(2,1)S(1)}, bf16[8,2,256,128]{3,2,1,0:T(8,128)(2,1)S(1)}, u32[]{:S(2)}, u32[]{:S(2)}) collective-permute-start(bf16[8,2,256,128]{3,2,1,0:T(8,128)(2,1)S(1)} %collective-permute-done.1.refs_8_), channel_id=1, source_target_pairs={{0,2},{2,4},{4,6},{6,8},{8,10},{10,12},{12,14},{14,16},{16,18},{18... | collective-permute-start | bytes 3145736 | tf_op jit(solution)/shard_map/ppermute | solution.py:24
  46.6 16.3 %copy-start.7 = (bf16[8,2,256,128]{3,2,1,0:T(8,128)(2,1)}, bf16[8,2,256,128]{3,2,1,0:T(8,128)(2,1)S(1)}, u32[]{:S(2)}) copy-start(bf16[8,2,256,128]{3,2,1,0:T(8,128)(2,1)S(1)} %collective-permute-done.2.refs_7_) | copy-start | bytes 3145732
  46.6 16.3 %collective-permute-start.3 = (bf16[8,2,256,128]{3,2,1,0:T(8,128)(2,1)S(1)}, bf16[8,2,256,128]{3,2,1,0:T(8,128)(2,1)S(1)}, u32[]{:S(2)}, u32[]{:S(2)}) collective-permute-start(bf16[8,2,256,128]{3,2,1,0:T(8,128)(2,1)S(1)} %collective-permute-done.2.refs_7_), channel_id=1, source_target_pairs={{0,2},{2,4},{4,6},{6,8},{8,10},{10,12},{12,14},{14,16},{16,18},{18... | collective-permute-start | bytes 3145736 | tf_op jit(solution)/shard_map/ppermute | solution.py:24
  62.9 1.0 copy-start.8
  89.6 34.6 %copy-start.1 = (bf16[8,2,256,128]{3,2,1,0:T(8,128)(2,1)S(1)}, bf16[8,2,256,128]{3,2,1,0:T(8,128)(2,1)}, u32[]{:S(2)}) copy-start(bf16[8,2,256,128]{3,2,1,0:T(8,128)(2,1)} %get-tuple-element.18) | copy-start | bytes 3145732
  89.6 16.1 %collective-permute-start.4 = (bf16[8,2,256,128]{3,2,1,0:T(8,128)(2,1)}, bf16[8,2,256,128]{3,2,1,0:T(8,128)(2,1)S(1)}, u32[]{:S(2)}, u32[]{:S(2)}) collective-permute-start(bf16[8,2,256,128]{3,2,1,0:T(8,128)(2,1)} %get-tuple-element.16), channel_id=1, source_target_pairs={{2,0},{4,2},{6,4},{8,6},{10,8},{12,10},{14,12},{16,14},{18,16},{20... | collective-permute-start | bytes 3145736 | tf_op jit(solution)/shard_map/ppermute | solution.py:24
  107.2 33.6 %copy-start = (bf16[8,2,256,128]{3,2,1,0:T(8,128)(2,1)S(1)}, bf16[8,2,256,128]{3,2,1,0:T(8,128)(2,1)}, u32[]{:S(2)}) copy-start(bf16[8,2,256,128]{3,2,1,0:T(8,128)(2,1)} %get-tuple-element.19) | copy-start | bytes 3145732
  107.2 17.0 %collective-permute-start.5 = (bf16[8,2,256,128]{3,2,1,0:T(8,128)(2,1)S(1)}, bf16[8,2,256,128]{3,2,1,0:T(8,128)(2,1)S(1)}, u32[]{:S(2)}, u32[]{:S(2)}) collective-permute-start(bf16[8,2,256,128]{3,2,1,0:T(8,128)(2,1)S(1)} %add_convert_fusion.2), channel_id=1, source_target_pairs={{2,0},{4,2},{6,4},{8,6},{10,8},{12,10},{14,12},{16,14},{18,16},{20... | collective-permute-start | bytes 3145736 | tf_op jit(solution)/shard_map/ppermute | solution.py:24
  124.5 17.9 %copy-start.2 = (bf16[256,2048]{1,0:T(8,128)(2,1)S(1)}, bf16[256,2048]{1,0:T(8,128)(2,1)}, u32[]{:S(2)}) copy-start(bf16[256,2048]{1,0:T(8,128)(2,1)} %get-tuple-element.15) | copy-start | bytes 3145732
  124.5 16.2 %collective-permute-start.6 = (bf16[8,2,256,128]{3,2,1,0:T(8,128)(2,1)S(1)}, bf16[8,2,256,128]{3,2,1,0:T(8,128)(2,1)S(1)}, u32[]{:S(2)}, u32[]{:S(2)}) collective-permute-start(bf16[8,2,256,128]{3,2,1,0:T(8,128)(2,1)S(1)} %add_convert_fusion.1), channel_id=1, source_target_pairs={{2,0},{4,2},{6,4},{8,6},{10,8},{12,10},{14,12},{16,14},{18,16},{20... | collective-permute-start | bytes 3145736 | tf_op jit(solution)/shard_map/ppermute | solution.py:24
  140.8 2.9 %copy-start.10 = (f32[8,8,128]{2,1,0:T(8,128)S(1)}, f32[8,8,128]{2,1,0:T(8,128)}, u32[]{:S(2)}) copy-start(f32[8,8,128]{2,1,0:T(8,128)} %get-tuple-element.23) | copy-start | bytes 98308
  141.2 16.1 %collective-permute-start.7 = (bf16[8,2,256,128]{3,2,1,0:T(8,128)(2,1)S(1)}, bf16[8,2,256,128]{3,2,1,0:T(8,128)(2,1)S(1)}, u32[]{:S(2)}, u32[]{:S(2)}) collective-permute-start(bf16[8,2,256,128]{3,2,1,0:T(8,128)(2,1)S(1)} %add_convert_fusion), channel_id=1, source_target_pairs={{2,0},{4,2},{6,4},{8,6},{10,8},{12,10},{14,12},{16,14},{18,16},{20... | collective-permute-start | bytes 3145736 | tf_op jit(solution)/shard_map/ppermute | solution.py:24
  157.3 1.0 copy-start.9
  162.6 3.9 %copy-start.11 = (f32[8,128]{1,0:T(8,128)S(1)}, f32[8,128]{1,0:T(8,128)}, u32[]{:S(2)}) copy-start(f32[8,128]{1,0:T(8,128)} %get-tuple-element.24) | copy-start | bytes 12292
where the time goes:
time: 225 us; the launch traced here: 224 us
  waiting for transfers between devices  65.4 us (29%)
  blocking collectives  57.4 us (26%)
  starting transfers between devices  49.8 us (22%)
  Pallas kernels  33.5 us (15%)
  local copies, waits for them, and re-layouts  12.5 us (6%)
  other arithmetic  4.93 us (2%)
    ppermute x8, waiting for transfers between devices, hop(): lax.ppermute(value, axis, [(source, source + step) for source in range(in...  65.4 us
    psum x1, blocking collectives, body(): gains = lax.psum(parts, ('seq', 'kv'))  57.4 us
    ppermute x8, starting transfers between devices, hop(): lax.ppermute(value, axis, [(source, source + step) for source in range(in...  49.8 us
    pallas_call x1, Pallas kernels, body(): pl.pallas_call(functools.partial(attn_kernel, blocks, group), grid=(kv_he...  25.7 us
    unnamed x29, local copies, waits for them, and re-layouts  7.62 us
  transfers between devices with their start and end apart: 8, of which 7 were waited for; matrix products, arithmetic and copies ran while one was open for 2% of the time, Pallas kernels for 0%

commit v1 on v0

v1 whole, which is shorter than its diff:
```python
import functools
import math

import jax
import jax.numpy as jnp
from jax import lax
from jax.experimental import pallas as pl
from jax.experimental.pallas import tpu as pltpu
from jax.sharding import PartitionSpec as P

WINDOW_LENGTH = 1024

attn_scale = 168.0 ** (-0.5)
norm_eps = 1e-06
rope_base = 10000.0
log2_e = math.log2(math.e)
f32 = jnp.float32
bf16 = jnp.bfloat16


def rotary_tables(positions, head_width):
    half_width = head_width // 2
    frequency = rope_base ** (-(jnp.arange(half_width, dtype=f32) * 2.0) / head_width)
    angles = positions.astype(f32)[:, None] * frequency[None, :]
    cos, sin = jnp.cos(angles), jnp.sin(angles)
    return (jnp.concatenate([cos, cos], axis=-1), jnp.concatenate([-sin, sin], axis=-1))


def swap_halves(x):
    half = x.shape[-1] // 2
    return jnp.concatenate([x[:, half:], x[:, :half]], axis=-1)


def normalize(x, gain):
    x = x.astype(f32)
    inv = lax.rsqrt(jnp.mean(x * x, axis=-1, keepdims=True) + norm_eps)
    unit = x * inv
    return unit, inv, unit * gain


def norm_back(rot_grad, unit, inv, gain, cos, sin):
    grad = rot_grad * cos - swap_halves(rot_grad) * sin
    grad_unit = grad * gain
    out = inv * (grad_unit - unit * jnp.mean(grad_unit * unit, axis=-1, keepdims=True))
    part = grad * unit
    return out, jnp.sum(part.reshape(part.shape[0] // 8, 8, part.shape[1]), axis=0)


def dot(a, b, ca, cb):
    return lax.dot_general(a, b, (((ca,), (cb,)), ((), ())), preferred_element_type=f32)


def fused_kernel(
    n_seq, n_kv, reach, group,
    q_ref, do_ref, k_ref, v_ref, low_ref, qg_ref, kg_ref, cos_ref, sin_ref,
    dq_ref, dk_ref, dv_ref, gains_ref,
    kvbuf, tbuf, rbuf, own, e_scr, gw_scr, part_scr, gbuf, gstage,
    kv_send, kv_recv, t_send, t_recv, g_send, g_recv,
):
    blocks = reach + 1
    lag = 3
    heads, rows, width = kvbuf.shape[1], kvbuf.shape[3], kvbuf.shape[4]
    wide = rows * group
    d = lax.axis_index("seq")
    x = lax.axis_index("kv")
    mesh_ids = pl.DeviceIdType.MESH

    partners = []
    step = 1
    while step < n_seq:
        up = lax.rem(lax.div(d, step), 2)
        partners.append((d + step - 2 * step * up, x))
        step *= 2
    step = 1
    while step < n_kv:
        up = lax.rem(lax.div(x, step), 2)
        partners.append((d, x + step - 2 * step * up))
        step *= 2

    barrier = pltpu.get_barrier_semaphore()
    for p in partners:
        pl.semaphore_signal(barrier, inc=1, device_id=p, device_id_type=mesh_ids)

    @pl.when(d > 0)
    def _():
        pl.semaphore_signal(barrier, inc=1, device_id=(d - 1, x), device_id_type=mesh_ids)

    @pl.when(d < n_seq - 1)
    def _():
        pl.semaphore_signal(barrier, inc=1, device_id=(d + 1, x), device_id_type=mesh_ids)

    @pl.when(d >= 4)
    def _():
        pl.semaphore_signal(barrier, inc=1, device_id=(d - 4, x), device_id_type=mesh_ids)

    @pl.when(d < n_seq - 4)
    def _():
        pl.semaphore_signal(barrier, inc=1, device_id=(d + 4, x), device_id_type=mesh_ids)

    def some(count):
        return lax.div(count + n_seq - 1, n_seq)

    after = n_seq - 1 - d
    peers = some(d) + some(after) + some(lax.div(d, 4)) + some(lax.div(after, 4))
    pl.semaphore_wait(barrier, len(partners) + peers)

    core = lax.rem(d, 2)
    high = lax.rem(lax.div(d, 2), 2)
    mate = d + 1 - 2 * core
    routes = [
        (0, 4, d + 4, d < n_seq - 4),
        (0, 2, d + 2, high == 0),
        (0, 1, d + 1, core == 0),
        (4, 3, d - 1, (core == 1) & (d >= 4)),
        (4, 2, d - 2, (high == 1) & (d >= 4)),
        (2, 3, d + 1, (core == 0) & (d >= 2)),
        (2, 1, d - 1, (core == 1) & (d >= 2)),
    ]

    def kv_copy(r, g):
        source, target, where, _ = routes[r]
        return pltpu.make_async_remote_copy(
            src_ref=kvbuf.at[source, g], dst_ref=kvbuf.at[target, g],
            send_sem=kv_send.at[r, g], recv_sem=kv_recv.at[target - 1, g],
            device_id=(where, x), device_id_type=mesh_ids,
        )

    def kv_start(r, g):
        @pl.when(routes[r][3])
        def _():
            kv_copy(r, g).start()

    def kv_wait(slot, g):
        pltpu.make_async_remote_copy(
            src_ref=kvbuf.at[0, g], dst_ref=kvbuf.at[slot, g],
            send_sem=kv_send.at[0, g], recv_sem=kv_recv.at[slot - 1, g],
            device_id=(mate, x), device_id_type=mesh_ids,
        ).wait_recv()

    def term_copy(i, g):
        return pltpu.make_async_remote_copy(
            src_ref=tbuf.at[i, g], dst_ref=rbuf.at[i, g],
            send_sem=t_send.at[i, g], recv_sem=t_recv.at[i, g],
            device_id=(d - 1, x), device_id_type=mesh_ids,
        )

    def term_sends(i):
        return d >= reach - i

    def term_arrives(i):
        return (d >= reach - i - 1) & (d < n_seq - 1)

    for k in range(1, blocks):
        @pl.when(d < k)
        def _():
            kvbuf[k] = jnp.zeros(kvbuf.shape[1:], bf16)

    @pl.when(d == n_seq - 1)
    def _():
        rbuf[reach - 1] = jnp.zeros(rbuf.shape[1:], bf16)

    part_scr[...] = jnp.zeros(part_scr.shape, f32)

    def prep(g):
        cols = pl.ds(pl.multiple_of(g * width, width), width)
        _, _, normed = normalize(k_ref[:, cols], kg_ref[...])
        rot = normed * cos_ref[...] + swap_halves(normed) * sin_ref[...]
        kvbuf[0, g, 0] = rot.astype(bf16)
        kvbuf[0, g, 1] = v_ref[:, cols]

    def attend(g):
        cos, sin, gain = cos_ref[...], sin_ref[...], qg_ref[...]
        cols = [
            pl.ds(pl.multiple_of((g * group + h) * width, width), width) for h in range(group)
        ]
        rots = []
        for h in range(group):
            _, _, normed = normalize(q_ref[:, cols[h]], gain)
            rots.append((normed * cos + swap_halves(normed) * sin).astype(bf16))
        q = jnp.concatenate(rots, axis=0)
        do = jnp.concatenate([do_ref[:, c] for c in cols], axis=0)
        low = low_ref[...]
        key_iota = lax.broadcasted_iota(jnp.int32, (rows, wide), 0)
        query_iota = lax.rem(lax.broadcasted_iota(jnp.int32, (1, wide), 1), rows)
        total = jnp.zeros((1, wide), f32)
        for j in range(blocks):
            s = dot(kvbuf[reach - j, g, 0], q, 1, 1)
            e = jnp.exp2(s * (attn_scale * log2_e))
            seen = key_iota >= low - j * rows
            if j == blocks - 1:
                seen = seen & (key_iota <= query_iota)
            e = jnp.where(seen, e, 0.0)
            total = total + jnp.sum(e, axis=0, keepdims=True)
            e_scr[j] = e
        inv_total = 1.0 / total
        delta = jnp.zeros((1, wide), f32)
        for j in range(blocks):
            w = e_scr[j] * inv_total
            wb = w.astype(bf16)
            gw = dot(kvbuf[reach - j, g, 1], do, 1, 1)
            delta = delta + jnp.sum(wb.astype(f32) * gw, axis=0, keepdims=True)
            gw_scr[j] = gw
            e_scr[j] = w
            term = dot(wb, do, 1, 0)
            if j < reach:
                tbuf[j, g, 1] = term.astype(bf16)
            else:
                own[g, 1] = term
        dq_t = jnp.zeros((width, wide), f32)
        for j in range(blocks):
            gs = (e_scr[j] * (gw_scr[j] - delta) * attn_scale).astype(bf16)
            dq_t = dq_t + dot(kvbuf[reach - j, g, 0], gs, 0, 0)
            term = dot(gs, q, 1, 0)
            if j < reach:
                tbuf[j, g, 0] = term.astype(bf16)
            else:
                own[g, 0] = term
        dq = dq_t.T
        for h in range(group):
            unit, inv, _ = normalize(q_ref[:, cols[h]], gain)
            out, p = norm_back(dq[h * rows : (h + 1) * rows], unit, inv, gain, cos, sin)
            dq_ref[:, cols[h]] = out.astype(bf16)
            part_scr[0] += p

    def finish(g):
        cols = pl.ds(pl.multiple_of(g * width, width), width)
        gain = kg_ref[...]
        unit, inv, _ = normalize(k_ref[:, cols], gain)
        dk = rbuf[reach - 1, g, 0].astype(f32) + own[g, 0]
        out, p = norm_back(dk, unit, inv, gain, cos_ref[...], sin_ref[...])
        dk_ref[:, cols] = out.astype(bf16)
        dv_ref[:, cols] = (rbuf[reach - 1, g, 1].astype(f32) + own[g, 1]).astype(bf16)
        part_scr[1] += p

    def turn(t, _):
        @pl.when(t < heads)
        def _():
            prep(t)

            for r in range(3):
                kv_start(r, t)

        g1 = t - 1

        @pl.when((g1 >= 0) & (g1 < heads))
        def _():
            @pl.when(d >= 4)
            def _():
                kv_wait(4, g1)
                kv_start(3, g1)
                kv_start(4, g1)

            @pl.when(high == 1)
            def _():
                kv_wait(2, g1)
                kv_start(5, g1)
                kv_start(6, g1)

        g2 = t - 2

        @pl.when((g2 >= 0) & (g2 < heads) & (high == 0) & (d >= 4))
        def _():
            kv_wait(2, g2)
            kv_start(5, g2)
            kv_start(6, g2)

        for i in range(1, reach):
            g = t - lag - i

            @pl.when((g >= 0) & (g < heads) & term_sends(i))
            def _():
                @pl.when(d < n_seq - 1)
                def _():
                    term_copy(i - 1, g).wait_recv()
                    tbuf[i, g] = (tbuf[i, g].astype(f32) + rbuf[i - 1, g].astype(f32)).astype(bf16)

                term_copy(i, g).start()

        g = t - lag

        @pl.when((g >= 0) & (g < heads))
        def _():
            @pl.when(d >= 1)
            def _():
                kv_wait(1, g)

            @pl.when(d >= 3)
            def _():
                kv_wait(3, g)

            attend(g)

            @pl.when(term_sends(0))
            def _():
                term_copy(0, g).start()

        f = t - lag - reach

        @pl.when((f >= 0) & (f < heads))
        def _():
            @pl.when(d < n_seq - 1)
            def _():
                term_copy(reach - 1, f).wait_recv()

            finish(f)

        return 0

    lax.fori_loop(0, heads + lag + reach, turn, 0)

    q_part = jnp.sum(part_scr[0], axis=0, keepdims=True)
    k_part = jnp.sum(part_scr[1], axis=0, keepdims=True)
    row = lax.broadcasted_iota(jnp.int32, (8, width), 0)
    total = jnp.where(row == 0, q_part, jnp.where(row == 1, k_part, 0.0))
    for r, p in enumerate(partners):
        gstage[r] = total
        copy = pltpu.make_async_remote_copy(
            src_ref=gstage.at[r], dst_ref=gbuf.at[r],
            send_sem=g_send.at[r], recv_sem=g_recv.at[r],
            device_id=p, device_id_type=mesh_ids,
        )
        copy.start()
        copy.wait()
        total = total + gbuf[r]
    gains_ref[...] = total

    def drain(g, _):
        for k in range(reach):
            @pl.when(term_sends(k))
            def _():
                term_copy(k, g).wait_send()

        for r in range(len(routes)):
            @pl.when(routes[r][3])
            def _():
                kv_copy(r, g).wait_send()

        return 0

    lax.fori_loop(0, heads, drain, 0)


def body(n_seq, n_kv, queries, keys, values, output_gradient, window_start, query_gain, key_gain):
    rows, q_heads, width = queries.shape
    kv_heads = keys.shape[1]
    group = q_heads // kv_heads
    reach = WINDOW_LENGTH // rows
    blocks = reach + 1
    first = lax.axis_index("seq") * rows
    cos, sin = rotary_tables(first + jnp.arange(rows, dtype=jnp.int32), width)
    low = jnp.tile(window_start - first + reach * rows, group)[None, :]
    q2 = queries.reshape(rows, q_heads * width)
    do2 = output_gradient.reshape(rows, q_heads * width)
    k2 = keys.reshape(rows, kv_heads * width)
    v2 = values.reshape(rows, kv_heads * width)
    rounds = (n_seq - 1).bit_length() + (n_kv - 1).bit_length()
    chunk = (kv_heads, 2, rows, width)
    dma = pltpu.SemaphoreType.DMA
    dq, dk, dv, gains = pl.pallas_call(
        functools.partial(fused_kernel, n_seq, n_kv, reach, group),
        out_shape=[
            jax.ShapeDtypeStruct(q2.shape, bf16),
            jax.ShapeDtypeStruct(k2.shape, bf16),
            jax.ShapeDtypeStruct(k2.shape, bf16),
            jax.ShapeDtypeStruct((8, width), f32),
        ],
        in_specs=[pl.BlockSpec(memory_space=pltpu.VMEM)] * 9,
        out_specs=[pl.BlockSpec(memory_space=pltpu.VMEM)] * 4,
        scratch_shapes=[
            pltpu.VMEM((blocks,) + chunk, bf16),
            pltpu.VMEM((reach,) + chunk, bf16),
            pltpu.VMEM((reach,) + chunk, bf16),
            pltpu.VMEM(chunk, f32),
            pltpu.VMEM((blocks, rows, rows * group), f32),
            pltpu.VMEM((blocks, rows, rows * group), f32),
            pltpu.VMEM((2, 8, width), f32),
            pltpu.VMEM((rounds, 8, width), f32),
            pltpu.VMEM((rounds, 8, width), f32),
        ]
        + [dma((7, kv_heads))]
        + [dma((reach, kv_heads))] * 3
        + [dma((rounds,))] * 2,
        compiler_params=pltpu.CompilerParams(
            collective_id=0, has_side_effects=True, vmem_limit_bytes=50 * 1024 * 1024
        ),
    )(q2, do2, k2, v2, low, query_gain[None, :], key_gain[None, :], cos, sin)
    return (
        dq.reshape(queries.shape),
        dk.reshape(keys.shape),
        dv.reshape(values.shape),
        gains[0],
        gains[1],
    )


def solution(mesh):
    split = P("seq", "kv", None)
    return jax.shard_map(
        functools.partial(body, mesh.shape["seq"], mesh.shape["kv"]),
        mesh=mesh,
        in_specs=(split, split, split, split, P("seq"), P(), P()),
        out_specs=(split, split, split, P(), P()),
        check_vma=False,
    )
```

time: 225 us -> 117 us (0.52)
  Pallas kernels: 33.5 us -> 106 us
  waiting for transfers between devices: 65.4 us -> 0 us
  blocking collectives: 57.4 us -> 0 us
  starting transfers between devices: 49.8 us -> 0 us
  other arithmetic: 4.93 us -> 0.75 us
  local copies, waits for them, and re-layouts: 12.5 us -> 8.64 us
    pallas_call x3 -> x1, Pallas kernels: 33.5 us -> 106 us  [body(): pl.pallas_call(functools.partial(fused_kernel, n_seq, n_kv, reach, group)...]
    ppermute x8 -> x0, waiting for transfers between devices: 65.4 us -> none  [hop(): lax.ppermute(value, axis, [(source, source + step) for source in range(in...]
    psum x1 -> x0, blocking collectives: 57.4 us -> none  [body(): gains = lax.psum(parts, ('seq', 'kv'))]
    ppermute x8 -> x0, starting transfers between devices: 49.8 us -> none  [hop(): lax.ppermute(value, axis, [(source, source + step) for source in range(in...]
    reshape x1, local copies, waits for them, and re-layouts: 2.53 us -> 0.2 us  [body(): v2 = values.reshape(rows, kv_heads * width)]
    unnamed x29 -> x19, local copies, waits for them, and re-layouts: 7.62 us -> 6.09 us
  transfers between devices with their start and end apart: 8 -> 0, of which waited for: 7 -> 0; matrix products, arithmetic and copies ran while one was open for 2% -> 0% of each run, Pallas kernels for 0% -> 0%
where the time goes in v1:
time: 117 us
  Pallas kernels  106 us (91%)
  local copies, waits for them, and re-layouts  8.64 us (7%)
    pallas_call x1, Pallas kernels, body(): pl.pallas_call(functools.partial(fused_kernel, n_seq, n_kv, reach, group)...  106 us
    unnamed x19, local copies, waits for them, and re-layouts  6.09 us

profile of v1, /device:TPU:0, one launch (start us, length us, event | category | flops | bytes accessed | tf_op | source)
XLA Modules:
  0.0 116.5 jit_solution(7105499889509676052)
XLA Ops:
  0.6 0.0 copy-start.6
  0.7 0.7 copy-done.6
  1.3 0.0 copy-start.4
  1.3 0.0 copy-start.5
  1.4 0.5 fusion
  1.9 0.1 pad_maximum_fusion.1.sin_ref
  2.0 0.1 pad_maximum_fusion.cos_ref
  2.1 0.3 copy-done.4
  2.4 0.2 copy-done.5
  2.5 0.0 copy-start.2
  2.5 0.0 copy-start.3
  2.5 0.2 copy_bitcast_fusion.2
  2.8 1.0 copy-done.2
  3.8 0.3 copy-done.3
  4.1 1.8 %copy_bitcast_fusion = (bf16[256,2048]{1,0:T(8,128)(2,1)}, bf16[256,2048]{1,0:T(8,128)(2,1)}) fusion(bf16[32,8,16,128]{3,2,1,0:T(8,128)(2,1)S(1)} %bitcast.35, bf16[32,8,16,128]{3,2,1,0:T(8,128)(2,1)S(1)} %bitcast.36), kind=kLoop, calls=%fused_computation | loop fusion | bytes 4194304 | tf_op jit(solution)/shard_map/reshape | solution.py:353
  5.9 0.0 copy-start
  5.9 0.0 copy-start.1
  5.9 0.7 copy-done
  6.6 0.0 copy-done.1
  6.6 106.5 %shard_map.110 = (bf16[256,2048]{1,0:T(8,128)(2,1)S(1)}, bf16[256,1024]{1,0:T(8,128)(2,1)S(1)}, bf16[256,1024]{1,0:T(8,128)(2,1)S(1)}, f32[8,128]{1,0:T(8,128)S(1)}) custom-call(bf16[256,2048]{1,0:T(8,128)(2,1)} %get-tuple-element.21.q_ref, bf16[256,2048]{1,0:T(8,128)(2,1)} %get-tuple-element.20.do_ref, bf16[256,1024]{1,0:T(8,128)(2,1)S(1)} %get-tuple-element.23.k_ref, ...), custom_call_target="tpu_custom_call" | custom-call | tf_op jit(solution)/shard_map/pallas_call | solution.py:359
  113.0 1.2 %copy.17 = bf16[32,8,16,128]{3,2,1,0:T(8,128)(2,1)} copy(bf16[32,8,16,128]{3,1,2,0:T(8,128)(2,1)S(1)} %bitcast.28) | data formatting | bytes 2097152
  114.2 0.9 copy.18
  115.1 0.5 slice_bitcast_fusion
  115.7 0.9 copy.19
  (4 shorter events, 0.0 us)
Async XLA Ops:
  0.6 0.7 copy-start.6
  1.3 1.0 copy-start.4
  1.3 1.2 %copy-start.5 = (bf16[256,8,128]{2,1,0:T(8,128)(2,1)S(1)}, bf16[256,8,128]{2,1,0:T(8,128)(2,1)}, u32[]{:S(2)}) copy-start(bf16[256,8,128]{2,1,0:T(8,128)(2,1)} %param.8) | copy-start | bytes 1572868
  2.5 1.2 %copy-start.2 = (bf16[256,16,128]{2,1,0:T(8,128)(2,1)S(1)}, bf16[256,16,128]{2,1,0:T(8,128)(2,1)}, u32[]{:S(2)}) copy-start(bf16[256,16,128]{2,1,0:T(8,128)(2,1)} %param.10) | copy-start | bytes 3145732
  2.5 1.5 %copy-start.3 = (bf16[256,16,128]{2,1,0:T(8,128)(2,1)S(1)}, bf16[256,16,128]{2,1,0:T(8,128)(2,1)}, u32[]{:S(2)}) copy-start(bf16[256,16,128]{2,1,0:T(8,128)(2,1)} %param.7) | copy-start | bytes 3145732
  5.9 0.7 copy-start
  5.9 0.7 copy-start.1

commit v2 on v1

--- a/solution.py
+++ b/solution.py
@@ -264,6 +264,24 @@
             kv_start(5, g2)
             kv_start(6, g2)
 
+        g = t - lag
+
+        @pl.when((g >= 0) & (g < heads))
+        def _():
+            @pl.when(d >= 1)
+            def _():
+                kv_wait(1, g)
+
+            @pl.when(d >= 3)
+            def _():
+                kv_wait(3, g)
+
+            attend(g)
+
+            @pl.when(term_sends(0))
+            def _():
+                term_copy(0, g).start()
+
         for i in range(1, reach):
             g = t - lag - i
 
@@ -275,24 +293,6 @@
                     tbuf[i, g] = (tbuf[i, g].astype(f32) + rbuf[i - 1, g].astype(f32)).astype(bf16)
 
                 term_copy(i, g).start()
-
-        g = t - lag
-
-        @pl.when((g >= 0) & (g < heads))
-        def _():
-            @pl.when(d >= 1)
-            def _():
-                kv_wait(1, g)
-
-            @pl.when(d >= 3)
-            def _():
-                kv_wait(3, g)
-
-            attend(g)
-
-            @pl.when(term_sends(0))
-            def _():
-                term_copy(0, g).start()
 
         f = t - lag - reach
 

time: 117 us -> 113 us (0.966)
  Pallas kernels: 106 us -> 103 us
    pallas_call x1, Pallas kernels: 106 us -> 103 us  [body(): pl.pallas_call(functools.partial(fused_kernel, n_seq, n_kv, reach, group)...]
where the time goes in v2:
time: 113 us
  Pallas kernels  103 us (91%)
  local copies, waits for them, and re-layouts  8.64 us (8%)
    pallas_call x1, Pallas kernels, body(): pl.pallas_call(functools.partial(fused_kernel, n_seq, n_kv, reach, group)...  103 us
    unnamed x19, local copies, waits for them, and re-layouts  6.09 us

profile of v2, /device:TPU:0, one launch (start us, length us, event | category | flops | bytes accessed | tf_op | source)
XLA Modules:
  0.0 113.0 jit_solution(2047620763564424364)
XLA Ops:
  0.6 0.0 copy-start.6
  0.7 0.7 copy-done.6
  1.3 0.0 copy-start.4
  1.3 0.0 copy-start.5
  1.4 0.5 fusion
  1.9 0.1 pad_maximum_fusion.1.sin_ref
  2.0 0.1 pad_maximum_fusion.cos_ref
  2.1 0.3 copy-done.4
  2.4 0.2 copy-done.5
  2.5 0.0 copy-start.2
  2.5 0.0 copy-start.3
  2.5 0.2 copy_bitcast_fusion.2
  2.8 1.0 copy-done.2
  3.8 0.3 copy-done.3
  4.1 1.8 %copy_bitcast_fusion = (bf16[256,2048]{1,0:T(8,128)(2,1)}, bf16[256,2048]{1,0:T(8,128)(2,1)}) fusion(bf16[32,8,16,128]{3,2,1,0:T(8,128)(2,1)S(1)} %bitcast.35, bf16[32,8,16,128]{3,2,1,0:T(8,128)(2,1)S(1)} %bitcast.36), kind=kLoop, calls=%fused_computation | loop fusion | bytes 4194304 | tf_op jit(solution)/shard_map/reshape | solution.py:353
  5.9 0.0 copy-start
  5.9 0.0 copy-start.1
  5.9 0.7 copy-done
  6.6 0.0 copy-done.1
  6.6 102.9 %shard_map.110 = (bf16[256,2048]{1,0:T(8,128)(2,1)S(1)}, bf16[256,1024]{1,0:T(8,128)(2,1)S(1)}, bf16[256,1024]{1,0:T(8,128)(2,1)S(1)}, f32[8,128]{1,0:T(8,128)S(1)}) custom-call(bf16[256,2048]{1,0:T(8,128)(2,1)} %get-tuple-element.21.q_ref, bf16[256,2048]{1,0:T(8,128)(2,1)} %get-tuple-element.20.do_ref, bf16[256,1024]{1,0:T(8,128)(2,1)S(1)} %get-tuple-element.23.k_ref, ...), custom_call_target="tpu_custom_call" | custom-call | tf_op jit(solution)/shard_map/pallas_call | solution.py:359
  109.5 1.2 %copy.17 = bf16[32,8,16,128]{3,2,1,0:T(8,128)(2,1)} copy(bf16[32,8,16,128]{3,1,2,0:T(8,128)(2,1)S(1)} %bitcast.28) | data formatting | bytes 2097152
  110.7 0.9 copy.18
  111.6 0.5 slice_bitcast_fusion
  112.1 0.9 copy.19
  (4 shorter events, 0.0 us)
Async XLA Ops:
  0.6 0.7 copy-start.6
  1.3 1.0 copy-start.4
  1.3 1.2 %copy-start.5 = (bf16[256,8,128]{2,1,0:T(8,128)(2,1)S(1)}, bf16[256,8,128]{2,1,0:T(8,128)(2,1)}, u32[]{:S(2)}) copy-start(bf16[256,8,128]{2,1,0:T(8,128)(2,1)} %param.8) | copy-start | bytes 1572868
  2.5 1.2 %copy-start.2 = (bf16[256,16,128]{2,1,0:T(8,128)(2,1)S(1)}, bf16[256,16,128]{2,1,0:T(8,128)(2,1)}, u32[]{:S(2)}) copy-start(bf16[256,16,128]{2,1,0:T(8,128)(2,1)} %param.10) | copy-start | bytes 3145732
  2.5 1.5 %copy-start.3 = (bf16[256,16,128]{2,1,0:T(8,128)(2,1)S(1)}, bf16[256,16,128]{2,1,0:T(8,128)(2,1)}, u32[]{:S(2)}) copy-start(bf16[256,16,128]{2,1,0:T(8,128)(2,1)} %param.7) | copy-start | bytes 3145732
  5.9 0.7 copy-start
  5.9 0.7 copy-start.1
